TPU v7x, 32 devices: a whole 2x2x4 slice. The times are simulated.
32 devices in a mesh: parts: 2 (over x), gx: 16 (over z, y, core).
Axes of the slice: x: 2, y: 2, z: 4, core: 2. Of those that a mesh axis runs over, the one named last changes fastest.
Arguments:
- potential: float32 [512, 32, 1024], P(('parts', 'gx')), parts along dimension 0, may hold values from -15 to 15
- surface_potential: float32 [512, 1024], P(('parts', 'gx')), parts along dimension 0, may hold values from -6 to 6
- elevation: float32 [512, 1024], P(('parts', 'gx')), parts along dimension 0, may hold values from -2.5 to 2.5
- vertical_coeff: float32 [512, 32, 1024], P(('parts', 'gx')), parts along dimension 0, may hold values from 2 to 16
- sigma_slope: float32 [512, 32, 1024], P(('parts', 'gx')), parts along dimension 0, may hold values from -0.8 to 0.8
- inverse_spacing: float32 [512, 1024], P(('parts', 'gx')), parts along dimension 0, may hold values from 0.5 to 2
- wet_tiles: int32 [4, 8], P('parts'), parts along dimension 0, may hold values 0 or 1
- hull_tiles: int32 [4, 8], P('parts'), parts along dimension 0, may hold values 0 or 1
- mooring_nodes: int32 [512], P('parts'), parts along dimension 0, may hold values from 0 to 262143
Outputs:
- new_potential: float32 [512, 32, 1024], P(('parts', 'gx')), parts along dimension 0
- new_elevation: float32 [512, 1024], P(('parts', 'gx')), parts along dimension 0
- new_surface_potential: float32 [512, 1024], P(('parts', 'gx')), parts along dimension 0
- defect_norms: float32 [8], P('parts'), parts along dimension 0
- node_values: float32 [4, 256], P('parts'), parts along dimension 0
There are 2 independent parts, one for each index of `parts`. A program takes and returns all parts, laid end to end along the dimension named above; each array names one. Nothing has to cross between parts.
All inputs are finite; a program needn't handle non-finite values.
Results may differ from a plain program's by a relative error of at most 0.0001.
Values sent between devices are 32-bit elements; how exact they have to be, the bound alone decides.
A program may use at most 128 MiB of HBM per device.

v0:
```python
import functools

import jax
import jax.numpy as jnp
from jax import lax
from jax.experimental import pallas as pl
from jax.experimental.pallas import tpu as pltpu
from jax.sharding import PartitionSpec as P

SWEEPS = 4
TILE = 128
SUB = 8
LANE = 128
GRAVITY = 9.81
SECTION_STEP = 0.05
K_UNROLL = 4
MESH = pl.DeviceIdType.MESH


def interior_blocks(rows):
    blocks = []
    start = 2
    while start < rows:
        size = min(7, rows - start)
        blocks.append(list(range(start, start + size)))
        start += size
    return blocks


def side_cells(cells, sub, lane):
    low = pltpu.roll(cells, 1, 1)
    low_wrap = jnp.where(sub == 0, 0.0, pltpu.roll(low, 1, 0))
    high = pltpu.roll(cells, LANE - 1, 1)
    high_wrap = jnp.where(sub == SUB - 1, 0.0, pltpu.roll(high, SUB - 1, 0))
    return (
        jnp.where(lane == 0, low_wrap, low),
        jnp.where(lane == LANE - 1, high_wrap, high),
    )


def kernel(
    count,
    rows,
    layers,
    pot_hbm,
    phis_hbm,
    elev_hbm,
    coeff_hbm,
    slope_hbm,
    spacing_hbm,
    wet_ref,
    hull_ref,
    nodes_ref,
    out_pot,
    out_elev,
    out_phis,
    out_norms,
    out_nodes,
    field,
    coeff,
    slope,
    inverse,
    ratio,
    value,
    spacing,
    new_elev,
    new_phis,
    norm_acc,
    payload,
    gathered,
    edge_sem,
    pot_sem,
    mat_sem,
    spacing_sem,
    out_sem,
    surf_sem,
    send_sem,
    recv_sem,
    all_send,
    all_recv,
):
    me = lax.axis_index("gx")
    last = count - 1
    groups = SUB
    barrier = pltpu.get_barrier_semaphore()

    @pl.loop(1, count)
    def _(t):
        pl.semaphore_signal(
            barrier, inc=1, device_id={"gx": lax.rem(me + t, count)}, device_id_type=MESH
        )

    def cols(j):
        return pl.ds(j * LANE, LANE)

    for j in range(groups):
        for x in (0, rows - 1):
            pltpu.make_async_copy(
                pot_hbm.at[x, :, cols(j)], field.at[0, x + 1, pl.ds(0, layers), j, :], edge_sem.at[0]
            ).start()
        pltpu.make_async_copy(
            phis_hbm.at[:, cols(j)], field.at[0, pl.ds(1, rows), layers, j, :], edge_sem.at[1]
        ).start()
        pltpu.make_async_copy(
            elev_hbm.at[:, cols(j)], field.at[0, pl.ds(1, rows), layers + 1, j, :], edge_sem.at[2]
        ).start()
    for j in range(groups):
        pltpu.make_async_copy(
            pot_hbm.at[pl.ds(1, rows - 2), :, cols(j)],
            field.at[0, pl.ds(2, rows - 2), pl.ds(0, layers), j, :],
            pot_sem,
        ).start()
    half = rows // 2
    for part in range(2):
        for j in range(groups):
            for which, (hbm, buf) in enumerate(((coeff_hbm, coeff), (slope_hbm, slope))):
                pltpu.make_async_copy(
                    hbm.at[pl.ds(part * half, half), :, cols(j)],
                    buf.at[pl.ds(part * half, half), :, j, :],
                    mat_sem.at[part, which],
                ).start()
    for j in range(groups):
        pltpu.make_async_copy(
            spacing_hbm.at[:, cols(j)], spacing.at[:, j, :], spacing_sem
        ).start()

    def wait_bytes(ref, sem):
        pltpu.make_async_copy(ref, ref, sem).wait()

    def wait_mats(part):
        for which, buf in enumerate((coeff, slope)):
            wait_bytes(buf.at[pl.ds(part * half, half)], mat_sem.at[part, which])

    zero = jnp.zeros((SUB, LANE), jnp.float32)

    @pl.when(me == 0)
    def _():
        @pl.loop(0, layers + 2)
        def _(k):
            field[0, 0, k] = zero
            field[1, 0, k] = zero

    @pl.when(me == last)
    def _():
        @pl.loop(0, layers + 2)
        def _(k):
            field[0, rows + 1, k] = zero
            field[1, rows + 1, k] = zero

    def exchange(turn):
        slot = turn % 2
        depth = layers + 2 if turn == 0 else layers
        left = pltpu.make_async_remote_copy(
            src_ref=field.at[slot, 1, pl.ds(0, depth)],
            dst_ref=field.at[slot, rows + 1, pl.ds(0, depth)],
            send_sem=send_sem.at[turn, 0],
            recv_sem=recv_sem.at[turn, 0],
            device_id={"gx": lax.max(me - 1, 0)},
            device_id_type=MESH,
        )
        right = pltpu.make_async_remote_copy(
            src_ref=field.at[slot, rows, pl.ds(0, depth)],
            dst_ref=field.at[slot, 0, pl.ds(0, depth)],
            send_sem=send_sem.at[turn, 1],
            recv_sem=recv_sem.at[turn, 1],
            device_id={"gx": lax.min(me + 1, last)},
            device_id_type=MESH,
        )
        return left, right

    def send(turn):
        left, right = exchange(turn)

        @pl.when(me > 0)
        def _():
            left.start()

        @pl.when(me < last)
        def _():
            right.start()

    def receive(turn):
        left, right = exchange(turn)

        @pl.when(me > 0)
        def _():
            left.wait_send()
            right.wait_recv()

        @pl.when(me < last)
        def _():
            right.wait_send()
            left.wait_recv()

    wait_bytes(pot_hbm.at[pl.ds(0, 2)], edge_sem.at[0])
    wait_bytes(phis_hbm, edge_sem.at[1])
    wait_bytes(elev_hbm, edge_sem.at[2])
    pl.semaphore_wait(barrier, count - 1)
    send(0)

    sub = lax.broadcasted_iota(jnp.int32, (SUB, LANE), 0)
    lane = lax.broadcasted_iota(jnp.int32, (SUB, LANE), 1)

    def forward(sweep, xs):
        src = sweep % 2
        first = sweep == 0
        near = sorted({x + d for x in xs for d in (-1, 0, 1)})

        def body(k, carry):
            now, q_below, q_now, flux_below, term, extra, acc = carry
            above = {x: field[src, x, k + 1] for x in near}
            q_above, flux, terms, extras = [], [], [], []
            for i, x in enumerate(xs):
                at = dict(zip(near, now))
                c = coeff[x - 1, k]
                q = above[x + 1] - above[x - 1]
                f = c * (above[x] - at[x])
                low, high = side_cells(at[x], sub, lane)
                s = slope[x - 1, k]
                if first:
                    s = 0.25 * s
                    slope[x - 1, k] = s
                r = (
                    (at[x + 1] + at[x - 1])
                    + (low + high)
                    - 4.0 * at[x]
                    + (f - flux_below[i])
                    + s * (q - q_below[i])
                )
                acc = acc + r * r
                if first:
                    inv = 1.0 / ((4.0 + c) + extra[i])
                    g = c * inv
                    inverse[x - 1, k] = inv
                    ratio[x - 1, k] = g
                    extras.append(c - c * g)
                else:
                    inv = inverse[x - 1, k]
                v = (r + term[i]) * inv
                value[x - 1, k] = v
                q_above.append(q)
                flux.append(f)
                terms.append(c * v)
            return (
                [above[x] for x in near],
                q_now,
                q_above,
                flux,
                terms,
                extras if first else extra,
                acc,
            )

        now = [field[src, x, 0] for x in near]
        at = dict(zip(near, now))
        q0 = [at[x + 1] - at[x - 1] for x in xs]
        zeros = [zero for _ in xs]
        carry = (now, q0, q0, zeros, zeros, zeros if first else [], zero)
        carry = lax.fori_loop(0, layers, body, carry, unroll=K_UNROLL)
        norm_acc[sweep] += carry[-1]

    def backward(sweep, xs):
        src, dst = sweep % 2, (sweep + 1) % 2

        def body(i, carry):
            k = layers - 1 - i
            out = []
            for u, x in zip(carry, xs):
                u = value[x - 1, k] + ratio[x - 1, k] * u
                field[dst, x, k] = field[src, x, k] + u
                out.append(u)
            return out

        lax.fori_loop(0, layers, body, [zero for _ in xs], unroll=K_UNROLL)

    blocks = interior_blocks(rows)
    edges = [1, rows]
    norm_acc[...] = jnp.zeros_like(norm_acc)

    for sweep in range(SWEEPS):
        final = sweep == SWEEPS - 1
        if sweep == 0:
            wait_bytes(field.at[0, pl.ds(2, rows - 2), pl.ds(0, layers)], pot_sem)
        for number, xs in enumerate(blocks):
            if sweep == 0:
                if number == 0:
                    wait_mats(0)
                if number == 1:
                    wait_mats(1)
            forward(sweep, xs)
            if not final:
                backward(sweep, xs)
        receive(sweep)
        forward(sweep, edges)
        if not final:
            backward(sweep, edges)
            send(sweep + 1)
        if sweep == 0:
            for x in range(rows + 2):
                field[1, x, layers] = field[0, x, layers]

    tile_row = (me * rows) // TILE
    mask = jnp.zeros((SUB, LANE), jnp.int32)
    for j in range(groups):
        free = wet_ref[tile_row, j] * (1 - hull_ref[tile_row, j])
        mask = jnp.where(sub == j, free, mask)
    weight = SECTION_STEP * mask.astype(jnp.float32)
    wait_bytes(spacing, spacing_sem)

    @pl.loop(1, rows + 1)
    def _(x):
        elev = field[0, x, layers + 1]
        phis = field[0, x, layers]
        eta_dx = (field[0, x + 1, layers + 1] - field[0, x - 1, layers + 1]) * 0.5
        phis_dx = (field[0, x + 1, layers] - field[0, x - 1, layers]) * 0.5
        low, high = side_cells(elev, sub, lane)
        eta_dy = (high - low) * 0.5
        low, high = side_cells(phis, sub, lane)
        phis_dy = (high - low) * 0.5
        top = field[SWEEPS % 2 ^ 1, x, layers - 1] + value[x - 1, layers - 1]
        speed = (phis - top) * spacing[x - 1]
        factor = 1.0 + eta_dx * eta_dx + eta_dy * eta_dy
        eta_rate = speed * factor - (phis_dx * eta_dx + phis_dy * eta_dy)
        phis_rate = -GRAVITY * elev - 0.5 * (
            phis_dx * phis_dx + phis_dy * phis_dy - speed * speed * factor
        )
        new_elev[x - 1] = elev + weight * eta_rate
        new_phis[x - 1] = phis + weight * phis_rate

    for j in range(groups):
        for which, (buf, out) in enumerate(((new_elev, out_elev), (new_phis, out_phis))):
            pltpu.make_async_copy(buf.at[:, j, :], out.at[:, cols(j)], surf_sem.at[which]).start()

    local = nodes_ref[...] - me * (rows * groups * LANE)
    node_line = jnp.right_shift(local, 7)
    node_lane = jnp.bitwise_and(local, LANE - 1)
    node_count = local.shape[1]
    lines = rows * groups
    pick_line = (
        lax.broadcasted_iota(jnp.int32, (lines, node_count), 0) == node_line
    ).astype(jnp.float32)
    pick_lane = lax.broadcasted_iota(jnp.int32, (LANE, node_count), 0) == node_lane
    pieces = node_count // LANE
    for which, buf in enumerate((new_elev, new_phis)):
        found = lax.dot_general(
            buf[...].reshape(lines, LANE),
            pick_line,
            (((0,), (0,)), ((), ())),
            precision=lax.Precision.HIGHEST,
            preferred_element_type=jnp.float32,
        )
        found = jnp.sum(jnp.where(pick_lane, found, 0.0), axis=0, keepdims=True)
        for piece in range(pieces):
            line = which * pieces + piece
            payload[line : line + 1, :] = found[:, piece * LANE : (piece + 1) * LANE]
    for sweep in range(SWEEPS):
        line = 2 * pieces + sweep
        payload[line : line + 1, :] = jnp.sum(norm_acc[sweep], axis=0, keepdims=True)
    gathered[me] = payload[...]

    def share(t):
        return pltpu.make_async_remote_copy(
            src_ref=payload,
            dst_ref=gathered.at[me],
            send_sem=all_send.at[t],
            recv_sem=all_recv.at[me],
            device_id={"gx": lax.rem(me + t, count)},
            device_id_type=MESH,
        )

    @pl.loop(1, count)
    def _(t):
        share(t).start()

    for number, xs in enumerate(blocks + [edges]):
        backward(SWEEPS - 1, xs)
        spans = [(xs[0], len(xs))] if xs is not edges else [(x, 1) for x in xs]
        for start, size in spans:
            for j in range(groups):
                pltpu.make_async_copy(
                    field.at[SWEEPS % 2, pl.ds(start, size), pl.ds(0, layers), j, :],
                    out_pot.at[pl.ds(start - 1, size), :, cols(j)],
                    out_sem,
                ).start()

    @pl.loop(1, count)
    def _(t):
        source = lax.rem(me + t, count)
        pltpu.make_async_remote_copy(
            src_ref=payload,
            dst_ref=gathered.at[source],
            send_sem=all_send.at[t],
            recv_sem=all_recv.at[source],
            device_id={"gx": source},
            device_id_type=MESH,
        ).wait()

    total = lax.fori_loop(
        1, count, lambda i, total: total + gathered[i], gathered[0]
    )
    payload[...] = total
    for which in range(2):
        for piece in range(pieces):
            line = which * pieces + piece
            out_nodes[which : which + 1, piece * LANE : (piece + 1) * LANE] = payload[
                line : line + 1, :
            ]
    cells = rows * count * layers * groups * LANE
    for sweep in range(SWEEPS):
        line = 2 * pieces + sweep
        out_norms[sweep] = jnp.sum(payload[line : line + 1, :]) / cells

    for which, (buf, out) in enumerate(((new_elev, out_elev), (new_phis, out_phis))):
        wait_bytes(buf, surf_sem.at[which])
    wait_bytes(field.at[SWEEPS % 2, pl.ds(1, rows), pl.ds(0, layers)], out_sem)


def on_device(
    potential,
    surface_potential,
    elevation,
    vertical_coeff,
    sigma_slope,
    inverse_spacing,
    wet_tiles,
    hull_tiles,
    mooring_nodes,
):
    rows, layers, width = potential.shape
    count = lax.axis_size("gx")
    assert width == SUB * LANE and TILE == LANE and TILE % rows == 0
    node_count = mooring_nodes.shape[0]
    f32 = jnp.float32
    block = (rows, layers, SUB, LANE)
    hbm = pl.BlockSpec(memory_space=pl.ANY)
    smem = pl.BlockSpec(memory_space=pltpu.SMEM)
    vmem = pl.BlockSpec(memory_space=pltpu.VMEM)
    dma = pltpu.SemaphoreType.DMA
    outs = pl.pallas_call(
        functools.partial(kernel, count, rows, layers),
        out_shape=(
            jax.ShapeDtypeStruct(potential.shape, f32),
            jax.ShapeDtypeStruct(elevation.shape, f32),
            jax.ShapeDtypeStruct(elevation.shape, f32),
            jax.ShapeDtypeStruct((SWEEPS,), f32),
            jax.ShapeDtypeStruct((2, node_count), f32),
        ),
        in_specs=[hbm] * 6 + [smem, smem, vmem],
        out_specs=(hbm, hbm, hbm, smem, vmem),
        scratch_shapes=[
            pltpu.VMEM((2, rows + 2, layers + 2, SUB, LANE), f32),
            pltpu.VMEM(block, f32),
            pltpu.VMEM(block, f32),
            pltpu.VMEM(block, f32),
            pltpu.VMEM(block, f32),
            pltpu.VMEM(block, f32),
            pltpu.VMEM((rows, SUB, LANE), f32),
            pltpu.VMEM((rows, SUB, LANE), f32),
            pltpu.VMEM((rows, SUB, LANE), f32),
            pltpu.VMEM((SWEEPS, SUB, LANE), f32),
            pltpu.VMEM((SUB, LANE), f32),
            pltpu.VMEM((count, SUB, LANE), f32),
            dma((3,)),
            dma,
            dma((2, 2)),
            dma,
            dma,
            dma((2,)),
            dma((SWEEPS, 2)),
            dma((SWEEPS, 2)),
            dma((count,)),
            dma((count,)),
        ],
        compiler_params=pltpu.CompilerParams(
            collective_id=0, has_side_effects=True, vmem_limit_bytes=40 * 1024 * 1024
        ),
        name="flow_section",
    )(
        potential,
        surface_potential,
        elevation,
        vertical_coeff,
        sigma_slope,
        inverse_spacing,
        wet_tiles,
        hull_tiles,
        mooring_nodes.reshape(1, node_count),
    )
    return tuple(outs)


def solution(mesh):
    return jax.shard_map(
        on_device,
        mesh=mesh,
        in_specs=(
            P(("parts", "gx"), None, None),
            P(("parts", "gx"), None),
            P(("parts", "gx"), None),
            P(("parts", "gx"), None, None),
            P(("parts", "gx"), None, None),
            P(("parts", "gx"), None),
            P("parts", None),
            P("parts", None),
            P("parts"),
        ),
        out_specs=(
            P(("parts", "gx"), None, None),
            P(("parts", "gx"), None),
            P(("parts", "gx"), None),
            P("parts"),
            P("parts", None),
        ),
        check_vma=False,
    )
```

profile of v0, /device:TPU:0, one launch (start us, length us, event | category | flops | bytes accessed | tf_op | source)
XLA Modules:
  0.0 49.9 jit_solution(7741717356094534477)
XLA Ops:
  0.6 0.0 copy-start
  0.6 1.6 %copy-done = f32[16,32,1024]{2,1,0:T(8,128)S(1)} copy-done((f32[16,32,1024]{2,1,0:T(8,128)S(1)}, f32[16,32,1024]{2,1,0:T(8,128)}, u32[]{:S(2)}) %copy-start) | copy-done | bytes 2097176
  2.2 0.0 copy-start.1
  2.2 1.6 %copy-done.1 = f32[16,32,1024]{2,1,0:T(8,128)S(1)} copy-done((f32[16,32,1024]{2,1,0:T(8,128)S(1)}, f32[16,32,1024]{2,1,0:T(8,128)}, u32[]{:S(2)}) %copy-start.1) | copy-done | bytes 2097176
  3.8 0.0 copy-start.2
  3.8 1.6 %copy-done.2 = f32[16,32,1024]{2,1,0:T(8,128)S(1)} copy-done((f32[16,32,1024]{2,1,0:T(8,128)S(1)}, f32[16,32,1024]{2,1,0:T(8,128)}, u32[]{:S(2)}) %copy-start.2) | copy-done | bytes 2097176
  5.4 0.0 copy-start.3
  5.4 0.8 %copy-done.3 = f32[16,1024]{1,0:T(8,128)S(1)} copy-done((f32[16,1024]{1,0:T(8,128)S(1)}, f32[16,1024]{1,0:T(8,128)}, u32[]{:S(2)}) %copy-start.3) | copy-done | bytes 65560
  6.2 0.0 copy-start.4
  6.3 0.8 %copy-done.4 = f32[16,1024]{1,0:T(8,128)S(1)} copy-done((f32[16,1024]{1,0:T(8,128)S(1)}, f32[16,1024]{1,0:T(8,128)}, u32[]{:S(2)}) %copy-start.4) | copy-done | bytes 65560
  7.1 0.0 copy-start.5
  7.1 0.8 %copy-done.5 = f32[16,1024]{1,0:T(8,128)S(1)} copy-done((f32[16,1024]{1,0:T(8,128)S(1)}, f32[16,1024]{1,0:T(8,128)}, u32[]{:S(2)}) %copy-start.5) | copy-done | bytes 65560
  7.9 0.0 copy-start.6
  7.9 0.7 %copy-done.6 = s32[2,8]{1,0:T(2,128)S(1)} copy-done((s32[2,8]{1,0:T(2,128)S(1)}, s32[2,8]{1,0:T(2,128)}, u32[]{:S(2)}) %copy-start.6) | copy-done | bytes 88
  8.6 0.0 copy-start.7
  8.6 0.7 %copy-done.7 = s32[2,8]{1,0:T(2,128)S(1)} copy-done((s32[2,8]{1,0:T(2,128)S(1)}, s32[2,8]{1,0:T(2,128)}, u32[]{:S(2)}) %copy-start.7) | copy-done | bytes 88
  9.3 0.0 copy-start.8
  9.3 0.7 %copy-done.8 = s32[256]{0:T(256)S(1)} copy-done((s32[256]{0:T(256)S(1)}, s32[256]{0:T(256)}, u32[]{:S(2)}) %copy-start.8) | copy-done | bytes 1048
  10.0 36.2 %flow_section.1 = (f32[16,32,1024]{2,1,0:T(8,128)S(1)}, f32[16,1024]{1,0:T(8,128)S(1)}, f32[16,1024]{1,0:T(8,128)S(1)}, f32[4]{0:T(128)S(1)}, f32[2,256]{1,0:T(2,128)S(1)}) custom-call(f32[16,32,1024]{2,1,0:T(8,128)S(1)} %copy-done, f32[16,1024]{1,0:T(8,128)S(1)} %copy-done.3, f32[16,1024]{1,0:T(8,128)S(1)} %copy-done.4, f32[16,32,1024]{2,1,0:T(8,128)S(1)} %copy-done.1, ...), custom_call_target="tpu_custom_call" | custom-call | tf_op jit(solution)/shard_map/flow_section/pallas_call | solution.py:439
  46.2 1.3 %copy.19 = f32[16,32,1024]{2,1,0:T(8,128)} copy(f32[16,32,1024]{2,1,0:T(8,128)S(1)} %get-tuple-element.10) | data formatting | bytes 4194304
  47.5 0.6 %copy.20 = f32[16,1024]{1,0:T(8,128)} copy(f32[16,1024]{1,0:T(8,128)S(1)} %get-tuple-element.11) | data formatting | bytes 131072
  48.2 0.6 %copy.21 = f32[16,1024]{1,0:T(8,128)} copy(f32[16,1024]{1,0:T(8,128)S(1)} %get-tuple-element.12) | data formatting | bytes 131072
  48.8 0.5 %copy.22 = f32[4]{0:T(128)} copy(f32[4]{0:T(128)S(1)} %get-tuple-element.13) | data formatting | bytes 32
  49.3 0.6 %copy.23 = f32[2,256]{1,0:T(2,128)} copy(f32[2,256]{1,0:T(2,128)S(1)} %get-tuple-element.14) | data formatting | bytes 4096
Async XLA Ops:
  0.6 1.6 %copy-start = (f32[16,32,1024]{2,1,0:T(8,128)S(1)}, f32[16,32,1024]{2,1,0:T(8,128)}, u32[]{:S(2)}) copy-start(f32[16,32,1024]{2,1,0:T(8,128)} %pot_hbm.1) | copy-start | bytes 6291460
  2.2 1.6 %copy-start.1 = (f32[16,32,1024]{2,1,0:T(8,128)S(1)}, f32[16,32,1024]{2,1,0:T(8,128)}, u32[]{:S(2)}) copy-start(f32[16,32,1024]{2,1,0:T(8,128)} %coeff_hbm.1) | copy-start | bytes 6291460
  3.8 1.6 %copy-start.2 = (f32[16,32,1024]{2,1,0:T(8,128)S(1)}, f32[16,32,1024]{2,1,0:T(8,128)}, u32[]{:S(2)}) copy-start(f32[16,32,1024]{2,1,0:T(8,128)} %slope_hbm.1) | copy-start | bytes 6291460
  5.4 0.8 %copy-start.3 = (f32[16,1024]{1,0:T(8,128)S(1)}, f32[16,1024]{1,0:T(8,128)}, u32[]{:S(2)}) copy-start(f32[16,1024]{1,0:T(8,128)} %phis_hbm.1) | copy-start | bytes 196612
  6.2 0.8 %copy-start.4 = (f32[16,1024]{1,0:T(8,128)S(1)}, f32[16,1024]{1,0:T(8,128)}, u32[]{:S(2)}) copy-start(f32[16,1024]{1,0:T(8,128)} %elev_hbm.1) | copy-start | bytes 196612
  7.1 0.8 %copy-start.5 = (f32[16,1024]{1,0:T(8,128)S(1)}, f32[16,1024]{1,0:T(8,128)}, u32[]{:S(2)}) copy-start(f32[16,1024]{1,0:T(8,128)} %spacing_hbm.1) | copy-start | bytes 196612
  7.9 0.7 %copy-start.6 = (s32[2,8]{1,0:T(2,128)S(1)}, s32[2,8]{1,0:T(2,128)}, u32[]{:S(2)}) copy-start(s32[2,8]{1,0:T(2,128)} %wet_ref.1) | copy-start | bytes 196
  8.6 0.7 %copy-start.7 = (s32[2,8]{1,0:T(2,128)S(1)}, s32[2,8]{1,0:T(2,128)}, u32[]{:S(2)}) copy-start(s32[2,8]{1,0:T(2,128)} %hull_ref.1) | copy-start | bytes 196
  9.3 0.7 %copy-start.8 = (s32[256]{0:T(256)S(1)}, s32[256]{0:T(256)}, u32[]{:S(2)}) copy-start(s32[256]{0:T(256)} %param.17) | copy-start | bytes 3076
where the time goes:
time: 50.3 us; the launch traced here: 49.9 us
  Pallas kernels  36.2 us (72%)
  local copies, waits for them, and re-layouts  13 us (26%)
  between operations  0.66 us (1%)
    pallas_call x1, Pallas kernels, on_device(): pl.pallas_call(functools.partial(kernel, count, rows, layers), out_shape=...  36.2 us
    unnamed x23, local copies, waits for them, and re-layouts  13 us

commit v1 on v0

--- a/solution.py
+++ b/solution.py
@@ -13,7 +13,9 @@
 LANE = 128
 GRAVITY = 9.81
 SECTION_STEP = 0.05
-K_UNROLL = 4
+K_UNROLL = 8
+BLOCK_ROWS = 5
+VMEM_BYTES = 60 * 1024 * 1024
 MESH = pl.DeviceIdType.MESH
 
 
@@ -21,7 +23,7 @@
     blocks = []
     start = 2
     while start < rows:
-        size = min(7, rows - start)
+        size = min(BLOCK_ROWS, rows - start)
         blocks.append(list(range(start, start + size)))
         start += size
     return blocks
@@ -48,14 +50,13 @@
     coeff_hbm,
     slope_hbm,
     spacing_hbm,
-    wet_ref,
-    hull_ref,
-    nodes_ref,
-    out_pot,
-    out_elev,
-    out_phis,
-    out_norms,
-    out_nodes,
+    wet_hbm,
+    hull_hbm,
+    nodes_hbm,
+    last_pot,
+    new_elev,
+    new_phis,
+    sums,
     field,
     coeff,
     slope,
@@ -63,17 +64,17 @@
     ratio,
     value,
     spacing,
-    new_elev,
-    new_phis,
     norm_acc,
     payload,
     gathered,
+    wet_ref,
+    hull_ref,
+    nodes_ref,
+    small_sem,
     edge_sem,
     pot_sem,
     mat_sem,
     spacing_sem,
-    out_sem,
-    surf_sem,
     send_sem,
     recv_sem,
     all_send,
@@ -124,6 +125,15 @@
             spacing_hbm.at[:, cols(j)], spacing.at[:, j, :], spacing_sem
         ).start()
 
+    small = [
+        pltpu.make_async_copy(hbm, buf, small_sem.at[i])
+        for i, (hbm, buf) in enumerate(
+            ((wet_hbm, wet_ref), (hull_hbm, hull_ref), (nodes_hbm, nodes_ref))
+        )
+    ]
+    for copy in small:
+        copy.start()
+
     def wait_bytes(ref, sem):
         pltpu.make_async_copy(ref, ref, sem).wait()
 
@@ -207,22 +217,23 @@
         near = sorted({x + d for x in xs for d in (-1, 0, 1)})
 
         def body(k, carry):
-            now, q_below, q_now, flux_below, term, extra, acc = carry
+            now, sides, q_below, q_now, flux_below, term, extra, acc = carry
             above = {x: field[src, x, k + 1] for x in near}
-            q_above, flux, terms, extras = [], [], [], []
+            q_above, flux, terms, extras, sides_above = [], [], [], [], []
             for i, x in enumerate(xs):
                 at = dict(zip(near, now))
                 c = coeff[x - 1, k]
                 q = above[x + 1] - above[x - 1]
                 f = c * (above[x] - at[x])
-                low, high = side_cells(at[x], sub, lane)
+                low, high = side_cells(above[x], sub, lane)
+                sides_above.append(low + high)
                 s = slope[x - 1, k]
                 if first:
                     s = 0.25 * s
                     slope[x - 1, k] = s
                 r = (
                     (at[x + 1] + at[x - 1])
-                    + (low + high)
+                    + sides[i]
                     - 4.0 * at[x]
                     + (f - flux_below[i])
                     + s * (q - q_below[i])
@@ -236,13 +247,15 @@
                     extras.append(c - c * g)
                 else:
                     inv = inverse[x - 1, k]
-                v = (r + term[i]) * inv
-                value[x - 1, k] = v
+                    g = ratio[x - 1, k]
+                right = r + term[i]
+                value[x - 1, k] = right * inv
                 q_above.append(q)
                 flux.append(f)
-                terms.append(c * v)
+                terms.append(right * g)
             return (
                 [above[x] for x in near],
+                sides_above,
                 q_now,
                 q_above,
                 flux,
@@ -255,7 +268,11 @@
         at = dict(zip(near, now))
         q0 = [at[x + 1] - at[x - 1] for x in xs]
         zeros = [zero for _ in xs]
-        carry = (now, q0, q0, zeros, zeros, zeros if first else [], zero)
+        sides0 = []
+        for x in xs:
+            low, high = side_cells(at[x], sub, lane)
+            sides0.append(low + high)
+        carry = (now, sides0, q0, q0, zeros, zeros, zeros if first else [], zero)
         carry = lax.fori_loop(0, layers, body, carry, unroll=K_UNROLL)
         norm_acc[sweep] += carry[-1]
 
@@ -267,7 +284,10 @@
             out = []
             for u, x in zip(carry, xs):
                 u = value[x - 1, k] + ratio[x - 1, k] * u
-                field[dst, x, k] = field[src, x, k] + u
+                if sweep == SWEEPS - 1:
+                    last_pot[x - 1, k] = field[src, x, k] + u
+                else:
+                    field[dst, x, k] = field[src, x, k] + u
                 out.append(u)
             return out
 
@@ -277,16 +297,17 @@
     edges = [1, rows]
     norm_acc[...] = jnp.zeros_like(norm_acc)
 
+    loaded = [False, False]
     for sweep in range(SWEEPS):
         final = sweep == SWEEPS - 1
         if sweep == 0:
             wait_bytes(field.at[0, pl.ds(2, rows - 2), pl.ds(0, layers)], pot_sem)
-        for number, xs in enumerate(blocks):
+        for xs in blocks:
             if sweep == 0:
-                if number == 0:
-                    wait_mats(0)
-                if number == 1:
-                    wait_mats(1)
+                for part in range(2):
+                    if part * half < xs[-1] and not loaded[part]:
+                        wait_mats(part)
+                        loaded[part] = True
             forward(sweep, xs)
             if not final:
                 backward(sweep, xs)
@@ -299,6 +320,8 @@
             for x in range(rows + 2):
                 field[1, x, layers] = field[0, x, layers]
 
+    for copy in small:
+        copy.wait()
     tile_row = (me * rows) // TILE
     mask = jnp.zeros((SUB, LANE), jnp.int32)
     for j in range(groups):
@@ -326,10 +349,6 @@
         )
         new_elev[x - 1] = elev + weight * eta_rate
         new_phis[x - 1] = phis + weight * phis_rate
-
-    for j in range(groups):
-        for which, (buf, out) in enumerate(((new_elev, out_elev), (new_phis, out_phis))):
-            pltpu.make_async_copy(buf.at[:, j, :], out.at[:, cols(j)], surf_sem.at[which]).start()
 
     local = nodes_ref[...] - me * (rows * groups * LANE)
     node_line = jnp.right_shift(local, 7)
@@ -372,16 +391,8 @@
     def _(t):
         share(t).start()
 
-    for number, xs in enumerate(blocks + [edges]):
+    for xs in blocks + [edges]:
         backward(SWEEPS - 1, xs)
-        spans = [(xs[0], len(xs))] if xs is not edges else [(x, 1) for x in xs]
-        for start, size in spans:
-            for j in range(groups):
-                pltpu.make_async_copy(
-                    field.at[SWEEPS % 2, pl.ds(start, size), pl.ds(0, layers), j, :],
-                    out_pot.at[pl.ds(start - 1, size), :, cols(j)],
-                    out_sem,
-                ).start()
 
     @pl.loop(1, count)
     def _(t):
@@ -395,24 +406,37 @@
             device_id_type=MESH,
         ).wait()
 
-    total = lax.fori_loop(
-        1, count, lambda i, total: total + gathered[i], gathered[0]
-    )
-    payload[...] = total
+    sums[...] = lax.fori_loop(1, count, lambda i, total: total + gathered[i], gathered[0])
+
+
+def unpack(
+    cells, last_pot, new_elev, new_phis, sums_in, out_pot, out_elev, out_phis, out_norms, out_nodes, sums, sem, sems
+):
+    small = pltpu.make_async_copy(sums_in, sums, sem)
+    small.start()
+    copies = []
+    for j in range(SUB):
+        cols = pl.ds(j * LANE, LANE)
+        copies += [
+            pltpu.make_async_copy(last_pot.at[:, :, j, :], out_pot.at[:, :, cols], sems.at[0, j]),
+            pltpu.make_async_copy(new_elev.at[:, j, :], out_elev.at[:, cols], sems.at[1, j]),
+            pltpu.make_async_copy(new_phis.at[:, j, :], out_phis.at[:, cols], sems.at[2, j]),
+        ]
+    for copy in copies:
+        copy.start()
+    small.wait()
+    pieces = out_nodes.shape[1] // LANE
     for which in range(2):
         for piece in range(pieces):
             line = which * pieces + piece
-            out_nodes[which : which + 1, piece * LANE : (piece + 1) * LANE] = payload[
+            out_nodes[which : which + 1, piece * LANE : (piece + 1) * LANE] = sums[
                 line : line + 1, :
             ]
-    cells = rows * count * layers * groups * LANE
     for sweep in range(SWEEPS):
         line = 2 * pieces + sweep
-        out_norms[sweep] = jnp.sum(payload[line : line + 1, :]) / cells
-
-    for which, (buf, out) in enumerate(((new_elev, out_elev), (new_phis, out_phis))):
-        wait_bytes(buf, surf_sem.at[which])
-    wait_bytes(field.at[SWEEPS % 2, pl.ds(1, rows), pl.ds(0, layers)], out_sem)
+        out_norms[sweep] = jnp.sum(sums[line : line + 1, :]) / cells
+    for copy in copies:
+        copy.wait()
 
 
 def on_device(
@@ -436,17 +460,17 @@
     smem = pl.BlockSpec(memory_space=pltpu.SMEM)
     vmem = pl.BlockSpec(memory_space=pltpu.VMEM)
     dma = pltpu.SemaphoreType.DMA
-    outs = pl.pallas_call(
+    surface = (rows, SUB, LANE)
+    results = pl.pallas_call(
         functools.partial(kernel, count, rows, layers),
         out_shape=(
-            jax.ShapeDtypeStruct(potential.shape, f32),
-            jax.ShapeDtypeStruct(elevation.shape, f32),
-            jax.ShapeDtypeStruct(elevation.shape, f32),
-            jax.ShapeDtypeStruct((SWEEPS,), f32),
-            jax.ShapeDtypeStruct((2, node_count), f32),
+            pltpu.VMEM(block, f32),
+            pltpu.VMEM(surface, f32),
+            pltpu.VMEM(surface, f32),
+            pltpu.VMEM((SUB, LANE), f32),
         ),
-        in_specs=[hbm] * 6 + [smem, smem, vmem],
-        out_specs=(hbm, hbm, hbm, smem, vmem),
+        in_specs=[hbm] * 9,
+        out_specs=(vmem,) * 4,
         scratch_shapes=[
             pltpu.VMEM((2, rows + 2, layers + 2, SUB, LANE), f32),
             pltpu.VMEM(block, f32),
@@ -454,25 +478,25 @@
             pltpu.VMEM(block, f32),
             pltpu.VMEM(block, f32),
             pltpu.VMEM(block, f32),
-            pltpu.VMEM((rows, SUB, LANE), f32),
-            pltpu.VMEM((rows, SUB, LANE), f32),
-            pltpu.VMEM((rows, SUB, LANE), f32),
+            pltpu.VMEM(surface, f32),
             pltpu.VMEM((SWEEPS, SUB, LANE), f32),
             pltpu.VMEM((SUB, LANE), f32),
             pltpu.VMEM((count, SUB, LANE), f32),
+            pltpu.SMEM(wet_tiles.shape, jnp.int32),
+            pltpu.SMEM(hull_tiles.shape, jnp.int32),
+            pltpu.VMEM((1, node_count), jnp.int32),
+            dma((3,)),
             dma((3,)),
             dma,
             dma((2, 2)),
             dma,
-            dma,
-            dma((2,)),
             dma((SWEEPS, 2)),
             dma((SWEEPS, 2)),
             dma((count,)),
             dma((count,)),
         ],
         compiler_params=pltpu.CompilerParams(
-            collective_id=0, has_side_effects=True, vmem_limit_bytes=40 * 1024 * 1024
+            collective_id=0, has_side_effects=True, vmem_limit_bytes=VMEM_BYTES
         ),
         name="flow_section",
     )(
@@ -486,6 +510,21 @@
         hull_tiles,
         mooring_nodes.reshape(1, node_count),
     )
+    outs = pl.pallas_call(
+        functools.partial(unpack, float(rows * count * layers * width)),
+        out_shape=(
+            jax.ShapeDtypeStruct(potential.shape, f32),
+            jax.ShapeDtypeStruct(elevation.shape, f32),
+            jax.ShapeDtypeStruct(elevation.shape, f32),
+            jax.ShapeDtypeStruct((SWEEPS,), f32),
+            jax.ShapeDtypeStruct((2, node_count), f32),
+        ),
+        in_specs=[hbm] * 4,
+        out_specs=(hbm, hbm, hbm, smem, vmem),
+        scratch_shapes=[pltpu.VMEM((SUB, LANE), f32), dma, dma((3, SUB))],
+        compiler_params=pltpu.CompilerParams(vmem_limit_bytes=8 * 1024 * 1024),
+        name="unpack",
+    )(*[pltpu.with_memory_space_constraint(r, pltpu.VMEM) for r in results])
     return tuple(outs)
 
 

time: 50.3 us -> 34.4 us (0.68)
  local copies, waits for them, and re-layouts: 13 us -> 0 us
  Pallas kernels: 36.2 us -> 33.6 us
    unnamed x23 -> x0, local copies, waits for them, and re-layouts: 13 us -> none
    pallas_call x1, Pallas kernels: 36.2 us -> 31.5 us  [on_device(): pl.pallas_call(functools.partial(kernel, count, rows, layers), out_shape=...]
    pallas_call x0 -> x1, Pallas kernels: none -> 2.18 us  [on_device(): pl.pallas_call(functools.partial(unpack, float(rows * count * layers * wi...]
where the time goes in v1:
time: 34.4 us; the launch traced here: 34.3 us
  Pallas kernels  33.6 us (98%)
  between operations  0.64 us (2%)
    pallas_call x1, Pallas kernels, on_device(): pl.pallas_call(functools.partial(kernel, count, rows, layers), out_shape=...  31.5 us
    pallas_call x1, Pallas kernels, on_device(): pl.pallas_call(functools.partial(unpack, float(rows * count * layers * wi...  2.18 us

profile of v1, /device:TPU:0, one launch (start us, length us, event | category | flops | bytes accessed | tf_op | source)
XLA Modules:
  0.0 34.3 jit_solution(18136091313898420794)
XLA Ops:
  0.6 31.5 %flow_section.1 = (f32[16,32,8,128]{3,2,1,0:T(8,128)S(1)}, f32[16,8,128]{2,1,0:T(8,128)S(1)}, f32[16,8,128]{2,1,0:T(8,128)S(1)}, f32[8,128]{1,0:T(8,128)S(1)}) custom-call(f32[16,32,1024]{2,1,0:T(8,128)} %pot_hbm.1, f32[16,1024]{1,0:T(8,128)} %phis_hbm.1, f32[16,1024]{1,0:T(8,128)} %elev_hbm.1, f32[16,32,1024]{2,1,0:T(8,128)} %coeff_hbm.1, ...), custom_call_target="tpu_custom_call" | custom-call | tf_op jit(solution)/shard_map/flow_section/pallas_call | solution.py:464
  32.1 2.2 %unpack.1 = (f32[16,32,1024]{2,1,0:T(8,128)}, f32[16,1024]{1,0:T(8,128)}, f32[16,1024]{1,0:T(8,128)}, f32[4]{0:T(128)}, f32[2,256]{1,0:T(2,128)}) custom-call(f32[16,32,8,128]{3,2,1,0:T(8,128)S(1)} %get-tuple-element.9.last_pot, f32[16,8,128]{2,1,0:T(8,128)S(1)} %get-tuple-element.10.new_elev, f32[16,8,128]{2,1,0:T(8,128)S(1)} %get-tuple-element.11.new_phis, ...), custom_call_target="tpu_custom_call" | custom-call | tf_op jit(solution)/shard_map/unpack/pallas_call | solution.py:513

commit v2 on v1

--- a/solution.py
+++ b/solution.py
@@ -14,6 +14,8 @@
 GRAVITY = 9.81
 SECTION_STEP = 0.05
 K_UNROLL = 8
+EDGE_UNROLL = 8
+HALVES = 2
 BLOCK_ROWS = 5
 VMEM_BYTES = 60 * 1024 * 1024
 MESH = pl.DeviceIdType.MESH
@@ -157,29 +159,30 @@
             field[0, rows + 1, k] = zero
             field[1, rows + 1, k] = zero
 
-    def exchange(turn):
+    def exchange(turn, part):
+        lines = pl.ds(part * (SUB // HALVES), SUB // HALVES)
         slot = turn % 2
         depth = layers + 2 if turn == 0 else layers
         left = pltpu.make_async_remote_copy(
-            src_ref=field.at[slot, 1, pl.ds(0, depth)],
-            dst_ref=field.at[slot, rows + 1, pl.ds(0, depth)],
-            send_sem=send_sem.at[turn, 0],
-            recv_sem=recv_sem.at[turn, 0],
+            src_ref=field.at[slot, 1, pl.ds(0, depth), lines],
+            dst_ref=field.at[slot, rows + 1, pl.ds(0, depth), lines],
+            send_sem=send_sem.at[turn, 0, part],
+            recv_sem=recv_sem.at[turn, 0, part],
             device_id={"gx": lax.max(me - 1, 0)},
             device_id_type=MESH,
         )
         right = pltpu.make_async_remote_copy(
-            src_ref=field.at[slot, rows, pl.ds(0, depth)],
-            dst_ref=field.at[slot, 0, pl.ds(0, depth)],
-            send_sem=send_sem.at[turn, 1],
-            recv_sem=recv_sem.at[turn, 1],
+            src_ref=field.at[slot, rows, pl.ds(0, depth), lines],
+            dst_ref=field.at[slot, 0, pl.ds(0, depth), lines],
+            send_sem=send_sem.at[turn, 1, part],
+            recv_sem=recv_sem.at[turn, 1, part],
             device_id={"gx": lax.min(me + 1, last)},
             device_id_type=MESH,
         )
         return left, right
 
-    def send(turn):
-        left, right = exchange(turn)
+    def send(turn, part):
+        left, right = exchange(turn, part)
 
         @pl.when(me > 0)
         def _():
@@ -189,8 +192,8 @@
         def _():
             right.start()
 
-    def receive(turn):
-        left, right = exchange(turn)
+    def receive(turn, part):
+        left, right = exchange(turn, part)
 
         @pl.when(me > 0)
         def _():
@@ -206,7 +209,8 @@
     wait_bytes(phis_hbm, edge_sem.at[1])
     wait_bytes(elev_hbm, edge_sem.at[2])
     pl.semaphore_wait(barrier, count - 1)
-    send(0)
+    for part in range(HALVES):
+        send(0, part)
 
     sub = lax.broadcasted_iota(jnp.int32, (SUB, LANE), 0)
     lane = lax.broadcasted_iota(jnp.int32, (SUB, LANE), 1)
@@ -276,6 +280,94 @@
         carry = lax.fori_loop(0, layers, body, carry, unroll=K_UNROLL)
         norm_acc[sweep] += carry[-1]
 
+    def edge_base(sweep):
+        src = sweep % 2
+
+        def body(k, carry):
+            now, sides, q_below, q_now, flux_below, extra = carry
+            above, sides_above, q_above, flux, extras = [], [], [], [], []
+            for i, (x, inner, sign) in enumerate(((1, 2, 1.0), (rows, rows - 1, -1.0))):
+                c = coeff[x - 1, k]
+                p = field[src, x, k + 1]
+                q = sign * field[src, inner, k + 1]
+                f = c * (p - now[i])
+                low, high = side_cells(p, sub, lane)
+                s = slope[x - 1, k]
+                if sweep == 0:
+                    s = 0.25 * s
+                    slope[x - 1, k] = s
+                    inv = 1.0 / ((4.0 + c) + extra[i])
+                    g = c * inv
+                    inverse[x - 1, k] = inv
+                    ratio[x - 1, k] = g
+                    extras.append(c - c * g)
+                value[x - 1, k] = (
+                    sign * q_now[i]
+                    + sides[i]
+                    - 4.0 * now[i]
+                    + (f - flux_below[i])
+                    + s * (q - q_below[i])
+                )
+                above.append(p)
+                sides_above.append(low + high)
+                q_above.append(q)
+                flux.append(f)
+            return above, sides_above, q_now, q_above, flux, extras
+
+        now = [field[src, x, 0] for x in (1, rows)]
+        sides0 = []
+        for cells in now:
+            low, high = side_cells(cells, sub, lane)
+            sides0.append(low + high)
+        q0 = [field[src, 2, 0], -field[src, rows - 1, 0]]
+        zeros = [zero, zero]
+        lax.fori_loop(
+            0,
+            layers,
+            body,
+            (now, sides0, q0, q0, zeros, zeros if sweep == 0 else []),
+            unroll=K_UNROLL,
+        )
+
+    def edge_rows(sweep, part):
+        src, dst = sweep % 2, (sweep + 1) % 2
+        size = SUB // HALVES
+        lines = pl.ds(part * size, size)
+        sides = ((1, 0, -1.0), (rows, rows + 1, 1.0))
+        empty = jnp.zeros((size, LANE), jnp.float32)
+
+        def down(k, carry):
+            h_below, h_now, term, acc = carry
+            h_above, terms = [], []
+            for i, (x, halo, sign) in enumerate(sides):
+                h = field[src, halo, k + 1, lines]
+                s = slope[x - 1, k, lines]
+                r = (value[x - 1, k, lines] + h_now[i]) + (sign * s) * (h - h_below[i])
+                acc = acc + r * r
+                right = r + term[i]
+                value[x - 1, k, lines] = right * inverse[x - 1, k, lines]
+                h_above.append(h)
+                terms.append(right * ratio[x - 1, k, lines])
+            return h_now, h_above, terms, acc
+
+        h0 = [field[src, halo, 0, lines] for _, halo, _ in sides]
+        carry = (h0, h0, [empty, empty], empty)
+        carry = lax.fori_loop(0, layers, down, carry, unroll=EDGE_UNROLL)
+        norm_acc[sweep, lines] += carry[-1]
+        if sweep == SWEEPS - 1:
+            return
+
+        def up(i, carry):
+            k = layers - 1 - i
+            out = []
+            for u, (x, _, _) in zip(carry, sides):
+                u = value[x - 1, k, lines] + ratio[x - 1, k, lines] * u
+                field[dst, x, k, lines] = field[src, x, k, lines] + u
+                out.append(u)
+            return out
+
+        lax.fori_loop(0, layers, up, [empty, empty], unroll=EDGE_UNROLL)
+
     def backward(sweep, xs):
         src, dst = sweep % 2, (sweep + 1) % 2
 
@@ -302,6 +394,8 @@
         final = sweep == SWEEPS - 1
         if sweep == 0:
             wait_bytes(field.at[0, pl.ds(2, rows - 2), pl.ds(0, layers)], pot_sem)
+        if sweep > 0:
+            edge_base(sweep)
         for xs in blocks:
             if sweep == 0:
                 for part in range(2):
@@ -311,11 +405,13 @@
             forward(sweep, xs)
             if not final:
                 backward(sweep, xs)
-        receive(sweep)
-        forward(sweep, edges)
-        if not final:
-            backward(sweep, edges)
-            send(sweep + 1)
+        if sweep == 0:
+            edge_base(0)
+        for part in range(HALVES):
+            receive(sweep, part)
+            edge_rows(sweep, part)
+            if not final:
+                send(sweep + 1, part)
         if sweep == 0:
             for x in range(rows + 2):
                 field[1, x, layers] = field[0, x, layers]
@@ -490,8 +586,8 @@
             dma,
             dma((2, 2)),
             dma,
-            dma((SWEEPS, 2)),
-            dma((SWEEPS, 2)),
+            dma((SWEEPS, 2, HALVES)),
+            dma((SWEEPS, 2, HALVES)),
             dma((count,)),
             dma((count,)),
         ],

time: 34.4 us -> 31.9 us (0.927)
  Pallas kernels: 33.6 us -> 31.1 us
    pallas_call x1, Pallas kernels: 31.5 us -> 28.9 us  [on_device(): pl.pallas_call(functools.partial(kernel, count, rows, layers), out_shape=...]
where the time goes in v2:
time: 31.9 us; the launch traced here: 31.7 us
  Pallas kernels  31.1 us (97%)
  between operations  0.64 us (2%)
    pallas_call x1, Pallas kernels, on_device(): pl.pallas_call(functools.partial(kernel, count, rows, layers), out_shape=...  28.9 us
    pallas_call x1, Pallas kernels, on_device(): pl.pallas_call(functools.partial(unpack, float(rows * count * layers * wi...  2.18 us

profile of v2, /device:TPU:0, one launch (start us, length us, event | category | flops | bytes accessed | tf_op | source)
XLA Modules:
  0.0 31.7 jit_solution(4945830268638244758)
XLA Ops:
  0.6 28.9 %flow_section.1 = (f32[16,32,8,128]{3,2,1,0:T(8,128)S(1)}, f32[16,8,128]{2,1,0:T(8,128)S(1)}, f32[16,8,128]{2,1,0:T(8,128)S(1)}, f32[8,128]{1,0:T(8,128)S(1)}) custom-call(f32[16,32,1024]{2,1,0:T(8,128)} %pot_hbm.1, f32[16,1024]{1,0:T(8,128)} %phis_hbm.1, f32[16,1024]{1,0:T(8,128)} %elev_hbm.1, f32[16,32,1024]{2,1,0:T(8,128)} %coeff_hbm.1, ...), custom_call_target="tpu_custom_call" | custom-call | tf_op jit(solution)/shard_map/flow_section/pallas_call | solution.py:560
  29.5 2.2 %unpack.1 = (f32[16,32,1024]{2,1,0:T(8,128)}, f32[16,1024]{1,0:T(8,128)}, f32[16,1024]{1,0:T(8,128)}, f32[4]{0:T(128)}, f32[2,256]{1,0:T(2,128)}) custom-call(f32[16,32,8,128]{3,2,1,0:T(8,128)S(1)} %get-tuple-element.9.last_pot, f32[16,8,128]{2,1,0:T(8,128)S(1)} %get-tuple-element.10.new_elev, f32[16,8,128]{2,1,0:T(8,128)S(1)} %get-tuple-element.11.new_phis, ...), custom_call_target="tpu_custom_call" | custom-call | tf_op jit(solution)/shard_map/unpack/pallas_call | solution.py:609
